TPU v7x, 256 devices: a whole 4x4x8 slice. The times are simulated.
256 devices in a mesh: vir: 32 (over x, z), occ: 4 (over y), rep: 2 (over core).
Axes of the slice: x: 4, y: 4, z: 8, core: 2. Of those that a mesh axis runs over, the one named last changes fastest.
Arguments:
- amplitudes: float32 [256, 64, 4096], P('vir', ('occ', 'rep')), may hold values from -6 to 6
- integrals: float32 [384, 512, 4096], P('vir', None, ('occ', 'rep')), may hold values from -0.005859375 to 0.005859375
- block_owner: int32 [256], replicated, may hold values from 0 to 31, as said below
Outputs:
- ladder: float32 [64, 512], P('occ', 'rep')
Inputs may be any that keep to these rules, and one draw needn't show every extreme that they name: `block_owner`: blocks 8 * s to 8 * s + 7 start on vir index s. No vir index owns more than 12 blocks and some owns exactly 12; slots beyond an index's count are unused. No vir index's starting blocks name one owner more than 2 times, and each names some owner exactly 2 times.
All inputs are finite; a program needn't handle non-finite values.
Results may differ from a plain program's by a relative error of at most 0.0001.
Values sent between devices are 32-bit elements; how exact they have to be, the bound alone decides.
No kernel may reach another device: no remote copies, remote signals or barrier semaphores. Data moves between devices by JAX's collectives and lax.ppermute only.
A program may use at most 128 MiB of HBM per device.

v0:
```python
import jax
import jax.numpy as jnp
from jax import lax
from jax.sharding import PartitionSpec as P


def block_ranks(owners, blocks_dev):
    block_ids = jnp.arange(owners.shape[0], dtype=jnp.int32)
    earlier = block_ids[None, :] < block_ids[:, None]
    same_owner = owners[None, :] == owners[:, None]
    same_source = block_ids[None, :] // blocks_dev == block_ids[:, None] // blocks_dev
    owner_rank = jnp.sum(jnp.where(same_owner & earlier, 1, 0), axis=1).astype(jnp.int32)
    src_rank = jnp.sum(jnp.where(same_owner & earlier & same_source, 1, 0), axis=1).astype(
        jnp.int32
    )
    return (owner_rank, src_rank)


def contract(owned, integrals):
    return jnp.einsum(
        "vpx,vax->pa",
        owned,
        integrals,
        precision=lax.Precision.HIGHEST,
        preferred_element_type=jnp.float32,
    )


def on_device(amplitudes, integrals, block_owner):
    vir_count = lax.axis_size("vir")
    blocks_dev = amplitudes.shape[0]
    slot_count = integrals.shape[0]
    capacity = max(2, 3 * blocks_dev // (2 * vir_count))
    vir_index = lax.axis_index("vir")
    owner_rank, src_rank = block_ranks(block_owner, blocks_dev)
    block_ids = jnp.arange(block_owner.shape[0], dtype=jnp.int32)
    is_mine = block_owner == vir_index
    slot_pick = is_mine[None, :] & (
        owner_rank[None, :] == jnp.arange(slot_count, dtype=jnp.int32)[:, None]
    )
    slot_live = jnp.sum(jnp.where(slot_pick, 1, 0), axis=1)
    chosen = jnp.sum(jnp.where(slot_pick, block_ids[None, :], 0), axis=1)
    flat_index = chosen // blocks_dev * capacity + src_rank[chosen]
    slot_mask = slot_live.astype(jnp.float32)[:, None, None]
    local_ids = vir_index * blocks_dev + jnp.arange(blocks_dev, dtype=jnp.int32)
    target = block_owner[local_ids]
    target_rank = src_rank[local_ids]
    target_hit = (
        target[None, None, :] == jnp.arange(vir_count, dtype=jnp.int32)[:, None, None]
    ) & (target_rank[None, None, :] == jnp.arange(capacity, dtype=jnp.int32)[None, :, None])
    send_index = jnp.sum(
        jnp.where(target_hit, jnp.arange(blocks_dev, dtype=jnp.int32)[None, None, :], 0), axis=2
    )
    send_live = jnp.sum(jnp.where(target_hit, 1, 0), axis=2).astype(jnp.float32)
    outgoing = jnp.take(amplitudes, send_index, axis=0) * send_live[:, :, None, None]
    arrived = lax.all_to_all(outgoing, "vir", split_axis=0, concat_axis=0, tiled=True)
    row_stack = arrived.reshape((arrived.shape[0] * arrived.shape[1],) + arrived.shape[2:])
    owned = jnp.take(row_stack, flat_index, axis=0) * slot_mask
    owned = lax.all_to_all(owned, ("occ", "rep"), split_axis=2, concat_axis=1, tiled=True)
    partial_value = contract(owned, integrals)
    rep_part = lax.psum_scatter(partial_value, "rep", scatter_dimension=1, tiled=True)
    pair_part = lax.psum_scatter(rep_part, "occ", scatter_dimension=0, tiled=True)
    return lax.psum(pair_part, "vir")


def solution(mesh):
    in_specs = (P("vir", ("occ", "rep"), None), P("vir", None, ("occ", "rep")), P())
    out_specs = P("occ", "rep")
    return jax.shard_map(
        on_device, mesh=mesh, in_specs=in_specs, out_specs=out_specs, check_vma=False
    )
```

profile of v0, /device:TPU:0, one launch (start us, length us, event | category | flops | bytes accessed | tf_op | source)
XLA Modules:
  0.0 531.7 jit_solution(18139110158587541731)
XLA Ops:
  6.5 0.0 copy-start
  6.6 1.0 select_reduce_fusion.1
  7.6 1.3 gather_fusion.1
  8.9 0.6 gather_fusion.2
  9.6 0.1 iota_compare_fusion.2
  9.7 0.1 fusion.8
  9.8 0.1 copy.20
  9.9 0.1 reshape.278
  10.0 0.1 copy.19
  10.1 0.1 copy.21
  10.2 0.0 copy-done
  10.2 4.3 gather_fusion.3
  14.5 8.5 %select_multiply_fusion = f32[32,2,8,4096]{3,2,1,0:T(8,128)} fusion(f32[32,2,8,4096]{3,2,1,0:T(8,128)} %bitcast.42, f32[32,2]{1,0:T(8,128)S(1)} %copy.21, pred[32,2]{1,0:T(8,128)(4,1)S(1)} %copy.19), kind=kLoop, calls=%fused_computation.5 | loop fusion | flops 4194304 | bytes 16777536 | tf_op jit(solution)/shard_map/mul | solution.py:55
  22.9 0.0 copy-start.2
  22.9 9.8 %all-to-all-start = ((f32[32,2,8,4096]{3,2,1,0:T(8,128)}), f32[32,2,8,4096]{3,2,1,0:T(8,128)}, u32[]{:S(2)}, u32[]{:S(2)}) async-start(f32[32,2,8,4096]{3,2,1,0:T(8,128)} %select_multiply_fusion), calls=%async_computation | async-start | bytes 16777216 | tf_op jit(solution)/shard_map/all_to_all | solution.py:56
  32.8 0.0 reduce-scatter.3.cloned.1.call-start
  32.8 0.0 copy-done.2
  32.9 0.1 select_reduce_fusion.2
  33.0 0.7 gather_fusion
  33.7 187.9 %all-to-all-done = f32[32,2,8,4096]{3,2,1,0:T(8,128)} async-done(((f32[32,2,8,4096]{3,2,1,0:T(8,128)}), f32[32,2,8,4096]{3,2,1,0:T(8,128)}, u32[]{:S(2)}, u32[]{:S(2)}) %all-to-all-start) | async-done | bytes 8388640 | tf_op jit(solution)/shard_map/all_to_all | solution.py:56
  221.6 5.3 gather_fusion.4
  226.9 1.6 select_multiply_fusion.1
  228.5 9.0 %copy.22 = f32[12,8,4096]{0,1,2:T(8,128)} copy(f32[12,8,4096]{2,1,0:T(8,128)S(1)} %select_multiply_fusion.1) | data formatting | bytes 3145728 | tf_op jit(solution)/shard_map/mul | solution.py:58
  237.5 18.2 %reshape.294 = f32[8,1,49152]{2,1,0:T(1,128)S(1)} reshape(f32[4096,8,12]{2,1,0:T(8,128)} %bitcast.40) | data formatting | bytes 3145728
  255.7 26.2 %all_to_all.23 = f32[8,1,49152]{2,1,0:T(1,128)} all-to-all(f32[8,1,49152]{2,1,0:T(1,128)S(1)} %reshape.294), channel_id=1, replica_groups=mesh['vir'=32,'occ'=4,'rep'=2] {'occ','rep'}, dimensions={0} | all-to-all | bytes 3145728 | tf_op jit(solution)/shard_map/all_to_all | solution.py:59
  281.9 0.5 broadcast.330
  282.4 5.8 %reduce = f32[8,49152]{1,0:T(8,128)S(1)} reduce(f32[8,1,49152]{2,1,0:T(1,128)} %all_to_all.23, f32[]{:T(128)} %broadcast.330), dimensions={1}, to_apply=%all_to_all.17.reduce_sub_computation | reduce | bytes 3145732 | tf_op jit(solution)/shard_map/all_to_all | solution.py:59
  288.2 24.4 %reshape.295 = f32[4096,8,12]{2,1,0:T(8,128)} reshape(f32[8,49152]{1,0:T(8,128)S(1)} %reduce) | data formatting | bytes 3145728
  312.6 0.0 copy-start.1
  312.6 10.2 %copy.23 = f32[12,8,8,512]{3,1,2,0:T(8,128)S(1)} copy(f32[12,8,8,512]{0,1,3,2:T(8,128)} %bitcast.41) | data formatting | bytes 3145728 | tf_op jit(solution)/shard_map/all_to_all | solution.py:59
  322.8 15.7 %fusion.2 = f32[64,512]{1,0:T(8,128)} fusion(f32[12,512,512]{2,1,0:T(8,128)} %param.4, f32[12,8,8,512]{3,1,2,0:T(8,128)S(1)} %copy.23), kind=kOutput, calls=%fused_computation.9 | convolution fusion | flops 2415919104 | bytes 14286848 | tf_op jit(solution)/shard_map/vpx,vax->pa/dot_general | solution.py:20
  338.5 0.0 reduce-scatter.3.cloned.1.call-update
  338.5 0.0 reduce-scatter.5.cloned.1.call-start
  338.6 16.5 %reduce-scatter.3.cloned.1.call-done = f32[64,256]{1,0:T(8,128)} async-done(((f32[64,512]{1,0:T(8,128)}), f32[64,256]{1,0:T(8,128)}) %reduce-scatter.3.cloned.1.call-update) | async-done | bytes 65552 | tf_op jit(solution)/shard_map/reduce_scatter | solution.py:61
  355.1 0.0 reduce-scatter.5.cloned.1.call-update
  355.1 26.6 %reduce-scatter.5.cloned.1.call-done = f32[16,256]{1,0:T(8,128)} async-done(((f32[64,256]{1,0:T(8,128)}), f32[16,256]{1,0:T(8,128)}) %reduce-scatter.5.cloned.1.call-update) | async-done | bytes 16400 | tf_op jit(solution)/shard_map/reduce_scatter | solution.py:62
  381.8 143.1 %psum.7 = f32[16,256]{1,0:T(8,128)} all-reduce(f32[16,256]{1,0:T(8,128)} %reduce-scatter.5.cloned.1.call-done), channel_id=1, replica_groups=mesh['vir'=32,'occ'=4,'rep'=2] {'vir'}, use_global_device_ids=true, to_apply=%region_8.9 | all-reduce | flops 4096 | bytes 32768 | tf_op jit(solution)/shard_map/psum | solution.py:63
  524.9 0.0 copy-done.1
  (15 shorter events, 0.1 us)
Async XLA Ops:
  6.5 3.6 copy-start
  22.9 9.9 %copy-start.2 = (s32[256]{0:T(256)S(1)}, s32[256]{0:T(256)}, u32[]{:S(2)}) copy-start(s32[256]{0:T(256)} %param.5) | copy-start | bytes 3076
  22.9 198.6 %all-to-all-start = ((f32[32,2,8,4096]{3,2,1,0:T(8,128)}), f32[32,2,8,4096]{3,2,1,0:T(8,128)}, u32[]{:S(2)}, u32[]{:S(2)}) async-start(f32[32,2,8,4096]{3,2,1,0:T(8,128)} %select_multiply_fusion), calls=%async_computation | async-start | bytes 16777216 | tf_op jit(solution)/shard_map/all_to_all | solution.py:56
  32.8 322.3 %reduce-scatter.3.cloned.1.call-start = ((), (), s32[]{:S(2)}) async-start(), calls=%async_computation.4 | async-start | bytes 196608 | tf_op jit(solution)/shard_map/reduce_scatter | solution.py:61
  312.6 212.3 %copy-start.1 = (f32[8,8,4096]{2,1,0:T(8,128)S(1)}, f32[8,8,4096]{2,1,0:T(8,128)}, u32[]{:S(2)}) copy-start(f32[8,8,4096]{2,1,0:T(8,128)} %param.3) | copy-start | bytes 3145732
  338.5 43.3 %reduce-scatter.5.cloned.1.call-start = ((), (), s32[]{:S(2)}) async-start(), calls=%async_computation.5 | async-start | bytes 81920 | tf_op jit(solution)/shard_map/reduce_scatter | solution.py:62
Sparse Core Ops, SparseCore 0:
  338.7 16.4 reduce-scatter.2
  357.6 24.1 reduce-scatter.4
where the time goes:
time: 532 us
  waiting for transfers between devices  231 us (43%)
  blocking collectives  169 us (32%)
  local copies, waits for them, and re-layouts  74.9 us (14%)
  other arithmetic  17.3 us (3%)
  matrix products  15.7 us (3%)
  between operations  13.5 us (3%)
  starting transfers between devices  9.92 us (2%)
    all_to_all x1, waiting for transfers between devices, on_device(): lax.all_to_all(outgoing, 'vir', split_axis=0, concat_axis=0, tiled=True)  188 us
    psum x1, blocking collectives, on_device(): return lax.psum(pair_part, 'vir')  143 us
    unnamed x8, local copies, waits for them, and re-layouts  42.6 us
    reduce_scatter x1, waiting for transfers between devices, on_device(): lax.psum_scatter(rep_part, 'occ', scatter_dimension=0, tiled=True)  26.6 us
    all_to_all x1, blocking collectives, on_device(): lax.all_to_all(owned, ('occ', 'rep'), split_axis=2, concat_axis=1, tiled=...  26.2 us
    reduce_scatter x1, waiting for transfers between devices, on_device(): lax.psum_scatter(partial_value, 'rep', scatter_dimension=1, tiled=True)  16.5 us
    dot_general x1, matrix products, contract(): jnp.einsum('vpx,vax->pa', owned, integrals, precision=lax.Precision.HIGHE...  15.7 us
    all_to_all x2, local copies, waits for them, and re-layouts, on_device(): lax.all_to_all(owned, ('occ', 'rep'), split_axis=2, concat_axis=1, tiled=...  10.7 us
  transfers between devices with their start and end apart: 3, of which 3 were waited for; matrix products, arithmetic and copies ran while one was open for 0% of the time, Pallas kernels for 0%

commit v1 on v0

--- a/solution.py
+++ b/solution.py
@@ -2,6 +2,17 @@
 import jax.numpy as jnp
 from jax import lax
 from jax.sharding import PartitionSpec as P
+
+
+def split_up(x, dim, size):
+    before, after = (x.shape[:dim], x.shape[dim + 1 :])
+    return jnp.moveaxis(x.reshape(*before, size, -1, *after), dim, 0)
+
+
+def laid_out(parts, dim):
+    lengths = list(parts.shape[1:])
+    lengths[dim] *= parts.shape[0]
+    return jnp.moveaxis(parts, 0, dim).reshape(lengths)
 
 
 def block_ranks(owners, blocks_dev):
@@ -56,7 +67,14 @@
     arrived = lax.all_to_all(outgoing, "vir", split_axis=0, concat_axis=0, tiled=True)
     row_stack = arrived.reshape((arrived.shape[0] * arrived.shape[1],) + arrived.shape[2:])
     owned = jnp.take(row_stack, flat_index, axis=0) * slot_mask
-    owned = lax.all_to_all(owned, ("occ", "rep"), split_axis=2, concat_axis=1, tiled=True)
+    length, index = (lax.axis_size(("occ", "rep")), lax.axis_index(("occ", "rep")))
+    blocks = split_up(owned, 2, length)
+    finished = [blocks[index]]
+    for step in range(1, length):
+        sent = blocks[index ^ step]
+        finished.append(lax.ppermute(sent, ("occ", "rep"), [(i, i ^ step) for i in range(length)]))
+    blocks = jnp.stack(finished)[index ^ jnp.arange(length)]
+    owned = laid_out(blocks, 1)
     partial_value = contract(owned, integrals)
     rep_part = lax.psum_scatter(partial_value, "rep", scatter_dimension=1, tiled=True)
     pair_part = lax.psum_scatter(rep_part, "occ", scatter_dimension=0, tiled=True)

time: 532 us -> 470 us (0.88)
  local copies, waits for them, and re-layouts: 74.9 us -> 20.8 us
  blocking collectives: 169 us -> 143 us
  waiting for transfers between devices: 231 us -> 246 us
  starting transfers between devices: 9.92 us -> 18.5 us
  other arithmetic: 17.3 us -> 11.2 us
    unnamed x8 -> x18, local copies, waits for them, and re-layouts: 42.6 us -> 4.91 us
    all_to_all x1 -> x0, blocking collectives: 26.2 us -> none  [on_device(): lax.all_to_all(owned, ('occ', 'rep'), split_axis=2, concat_axis=1, tiled=...]
    ppermute x0 -> x7, waiting for transfers between devices: none -> 13.6 us  [on_device(): lax.ppermute(sent, ('occ', 'rep'), [(i, i ^ step) for i in range(length)])]
    all_to_all x2 -> x0, local copies, waits for them, and re-layouts: 10.7 us -> none  [on_device(): lax.all_to_all(owned, ('occ', 'rep'), split_axis=2, concat_axis=1, tiled=...]
    mul x1 -> x0, local copies, waits for them, and re-layouts: 9.02 us -> none  [on_device(): owned = jnp.take(row_stack, flat_index, axis=0) * slot_mask]
    ppermute x0 -> x7, starting transfers between devices: none -> 8.54 us  [on_device(): lax.ppermute(sent, ('occ', 'rep'), [(i, i ^ step) for i in range(length)])]
    all_to_all x1 -> x0, other arithmetic: 5.79 us -> none  [on_device(): lax.all_to_all(owned, ('occ', 'rep'), split_axis=2, concat_axis=1, tiled=...]
  transfers between devices with their start and end apart: 3 -> 10, of which waited for: 3 -> 8; matrix products, arithmetic and copies ran while one was open for 0% -> 1% of each run, Pallas kernels for 0% -> 0%
where the time goes in v1:
time: 470 us; the launch traced here: 469 us
  waiting for transfers between devices  246 us (52%)
  blocking collectives  143 us (30%)
  local copies, waits for them, and re-layouts  20.8 us (4%)
  starting transfers between devices  18.5 us (4%)
  matrix products  15.7 us (3%)
  between operations  13.7 us (3%)
  other arithmetic  11.2 us (2%)
    all_to_all x1, waiting for transfers between devices, on_device(): lax.all_to_all(outgoing, 'vir', split_axis=0, concat_axis=0, tiled=True)  188 us
    psum x1, blocking collectives, on_device(): return lax.psum(pair_part, 'vir')  143 us
    reduce_scatter x1, waiting for transfers between devices, on_device(): lax.psum_scatter(rep_part, 'occ', scatter_dimension=0, tiled=True)  26.6 us
    reduce_scatter x1, waiting for transfers between devices, on_device(): lax.psum_scatter(partial_value, 'rep', scatter_dimension=1, tiled=True)  18.4 us
    dot_general x1, matrix products, contract(): jnp.einsum('vpx,vax->pa', owned, integrals, precision=lax.Precision.HIGHE...  15.7 us
    ppermute x7, waiting for transfers between devices, on_device(): lax.ppermute(sent, ('occ', 'rep'), [(i, i ^ step) for i in range(length)])  13.6 us
    all_to_all x1, starting transfers between devices, on_device(): lax.all_to_all(outgoing, 'vir', split_axis=0, concat_axis=0, tiled=True)  9.84 us
  transfers between devices with their start and end apart: 10, of which 8 were waited for; matrix products, arithmetic and copies ran while one was open for 1% of the time, Pallas kernels for 0%

profile of v1, /device:TPU:0, one launch (start us, length us, event | category | flops | bytes accessed | tf_op | source)
XLA Modules:
  0.0 469.3 jit_solution(16960705802244982749)
XLA Ops:
  6.6 1.0 select_reduce_fusion.1
  7.6 1.3 gather_fusion.1
  8.9 0.6 gather_fusion.2
  9.6 0.1 iota_compare_fusion.2
  9.7 0.1 fusion.10
  9.8 0.1 copy.12
  9.9 0.1 reshape.315
  10.0 0.1 copy.11
  10.1 0.1 copy.13
  10.2 4.3 gather_fusion.3
  14.5 8.5 %select_multiply_fusion = f32[32,2,8,4096]{3,2,1,0:T(8,128)} fusion(f32[32,2,8,4096]{3,2,1,0:T(8,128)} %bitcast.85, f32[32,2]{1,0:T(8,128)S(1)} %copy.13, pred[32,2]{1,0:T(8,128)(4,1)S(1)} %copy.11), kind=kLoop, calls=%fused_computation.6 | loop fusion | flops 4194304 | bytes 16777536 | tf_op jit(solution)/shard_map/mul | solution.py:66
  22.9 9.8 %all-to-all-start = ((f32[32,2,8,4096]{3,2,1,0:T(8,128)}), f32[32,2,8,4096]{3,2,1,0:T(8,128)}, u32[]{:S(2)}, u32[]{:S(2)}) async-start(f32[32,2,8,4096]{3,2,1,0:T(8,128)} %select_multiply_fusion), calls=%async_computation | async-start | bytes 16777216 | tf_op jit(solution)/shard_map/all_to_all | solution.py:67
  32.8 0.0 reduce-scatter.3.cloned.1.call-start
  32.9 0.1 select_reduce_fusion.2
  33.0 0.7 gather_fusion
  33.8 187.8 %all-to-all-done = f32[32,2,8,4096]{3,2,1,0:T(8,128)} async-done(((f32[32,2,8,4096]{3,2,1,0:T(8,128)}), f32[32,2,8,4096]{3,2,1,0:T(8,128)}, u32[]{:S(2)}, u32[]{:S(2)}) %all-to-all-start) | async-done | bytes 8388640 | tf_op jit(solution)/shard_map/all_to_all | solution.py:67
  221.6 4.0 gather_fusion.4
  225.6 1.3 fusion
  227.0 1.8 constant_dynamic-slice_fusion.7
  228.8 0.1 collective-permute-start
  228.9 1.7 collective-permute-start.1
  230.6 0.4 collective-permute-start.2
  231.0 3.3 collective-permute-start.3
  234.3 0.1 collective-permute-start.4
  234.4 0.7 bitcast_dynamic-update-slice_fusion
  235.1 0.0 collective-permute-done
  235.1 3.0 collective-permute-start.5
  238.0 0.7 bitcast_dynamic-update-slice_fusion.7
  238.7 0.1 collective-permute-start.6
  238.8 0.7 bitcast_dynamic-update-slice_fusion.6
  239.5 0.6 collective-permute-done.2
  240.1 0.7 bitcast_dynamic-update-slice_fusion.5
  240.8 6.9 %collective-permute-done.3 = f32[12,8,512]{2,1,0:T(8,128)S(1)} collective-permute-done((f32[12,8,512]{2,1,0:T(8,128)S(1)}, f32[12,8,512]{2,1,0:T(8,128)S(1)}, u32[]{:S(2)}, u32[]{:S(2)}) %collective-permute-start.3) | collective-permute-done | bytes 196640 | tf_op jit(solution)/shard_map/ppermute | solution.py:75
  247.7 0.7 bitcast_dynamic-update-slice_fusion.4
  248.4 2.7 collective-permute-done.4
  251.1 0.7 bitcast_dynamic-update-slice_fusion.3
  251.8 0.7 collective-permute-done.5
  252.4 0.7 bitcast_dynamic-update-slice_fusion.2
  253.1 2.7 collective-permute-done.6
  255.8 0.7 bitcast_dynamic-update-slice_fusion.1
  256.5 2.1 gather_fusion.5
  258.6 15.7 %fusion.4 = f32[64,512]{1,0:T(8,128)} fusion(f32[12,512,512]{2,1,0:T(8,128)} %param.4, f32[8,12,8,512]{3,2,1,0:T(8,128)S(1)} %gather_fusion.5), kind=kOutput, calls=%fused_computation.12 | convolution fusion | flops 2415919104 | bytes 14286848 | tf_op jit(solution)/shard_map/vpx,vax->pa/dot_general | solution.py:31
  274.3 0.0 reduce-scatter.3.cloned.1.call-update
  274.3 0.0 reduce-scatter.5.cloned.1.call-start
  274.4 18.4 %reduce-scatter.3.cloned.1.call-done = f32[64,256]{1,0:T(8,128)} async-done(((f32[64,512]{1,0:T(8,128)}), f32[64,256]{1,0:T(8,128)}) %reduce-scatter.3.cloned.1.call-update) | async-done | bytes 65552 | tf_op jit(solution)/shard_map/reduce_scatter | solution.py:79
  292.7 0.0 reduce-scatter.5.cloned.1.call-update
  292.8 26.6 %reduce-scatter.5.cloned.1.call-done = f32[16,256]{1,0:T(8,128)} async-done(((f32[64,256]{1,0:T(8,128)}), f32[16,256]{1,0:T(8,128)}) %reduce-scatter.5.cloned.1.call-update) | async-done | bytes 16400 | tf_op jit(solution)/shard_map/reduce_scatter | solution.py:80
  319.4 143.1 %psum.7 = f32[16,256]{1,0:T(8,128)} all-reduce(f32[16,256]{1,0:T(8,128)} %reduce-scatter.5.cloned.1.call-done), channel_id=1, replica_groups=mesh['vir'=32,'occ'=4,'rep'=2] {'vir'}, use_global_device_ids=true, to_apply=%region_8.9 | all-reduce | flops 4096 | bytes 32768 | tf_op jit(solution)/shard_map/psum | solution.py:81
  (29 shorter events, 0.2 us)
Async XLA Ops:
  6.5 3.6 copy-start
  22.9 9.9 %copy-start.1 = (s32[256]{0:T(256)S(1)}, s32[256]{0:T(256)}, u32[]{:S(2)}) copy-start(s32[256]{0:T(256)} %param.5) | copy-start | bytes 3076
  22.9 198.6 %all-to-all-start = ((f32[32,2,8,4096]{3,2,1,0:T(8,128)}), f32[32,2,8,4096]{3,2,1,0:T(8,128)}, u32[]{:S(2)}, u32[]{:S(2)}) async-start(f32[32,2,8,4096]{3,2,1,0:T(8,128)} %select_multiply_fusion), calls=%async_computation | async-start | bytes 16777216 | tf_op jit(solution)/shard_map/all_to_all | solution.py:67
  32.8 260.0 %reduce-scatter.3.cloned.1.call-start = ((), (), s32[]{:S(2)}) async-start(), calls=%async_computation.3 | async-start | bytes 196608 | tf_op jit(solution)/shard_map/reduce_scatter | solution.py:79
  228.8 6.3 %collective-permute-start = (f32[12,8,512]{2,1,0:T(8,128)S(1)}, f32[12,8,512]{2,1,0:T(8,128)S(1)}, u32[]{:S(2)}, u32[]{:S(2)}) collective-permute-start(f32[12,8,512]{2,1,0:T(8,128)S(1)} %bitcast.93), channel_id=1, source_target_pairs={{0,1},{1,0},{2,3},{3,2},{4,5},{5,4},{6,7},{7,6},{8,9},{9,8},{10,11... | collective-permute-start | bytes 589832 | tf_op jit(solution)/shard_map/ppermute | solution.py:75
  228.9 9.8 %collective-permute-start.1 = (f32[12,8,512]{2,1,0:T(8,128)S(1)}, f32[12,8,512]{2,1,0:T(8,128)S(1)}, u32[]{:S(2)}, u32[]{:S(2)}) collective-permute-start(f32[12,8,512]{2,1,0:T(8,128)S(1)} %bitcast.92), channel_id=1, source_target_pairs={{0,2},{1,3},{2,0},{3,1},{4,6},{5,7},{6,4},{7,5},{8,10},{9,11},{10,... | collective-permute-start | bytes 589832 | tf_op jit(solution)/shard_map/ppermute | solution.py:75
  230.6 9.5 %collective-permute-start.2 = (f32[12,8,512]{2,1,0:T(8,128)S(1)}, f32[12,8,512]{2,1,0:T(8,128)S(1)}, u32[]{:S(2)}, u32[]{:S(2)}) collective-permute-start(f32[12,8,512]{2,1,0:T(8,128)S(1)} %bitcast.91), channel_id=1, source_target_pairs={{0,3},{1,2},{2,1},{3,0},{4,7},{5,6},{6,5},{7,4},{8,11},{9,10},{10,... | collective-permute-start | bytes 589832 | tf_op jit(solution)/shard_map/ppermute | solution.py:75
  231.0 16.7 %collective-permute-start.3 = (f32[12,8,512]{2,1,0:T(8,128)S(1)}, f32[12,8,512]{2,1,0:T(8,128)S(1)}, u32[]{:S(2)}, u32[]{:S(2)}) collective-permute-start(f32[12,8,512]{2,1,0:T(8,128)S(1)} %bitcast.90), channel_id=1, source_target_pairs={{0,4},{1,5},{2,6},{3,7},{4,0},{5,1},{6,2},{7,3},{8,12},{9,13},{10,... | collective-permute-start | bytes 589832 | tf_op jit(solution)/shard_map/ppermute | solution.py:75
  234.3 16.8 %collective-permute-start.4 = (f32[12,8,512]{2,1,0:T(8,128)S(1)}, f32[12,8,512]{2,1,0:T(8,128)S(1)}, u32[]{:S(2)}, u32[]{:S(2)}) collective-permute-start(f32[12,8,512]{2,1,0:T(8,128)S(1)} %bitcast.89), channel_id=1, source_target_pairs={{0,5},{1,4},{2,7},{3,6},{4,1},{5,0},{6,3},{7,2},{8,13},{9,12},{10,... | collective-permute-start | bytes 589832 | tf_op jit(solution)/shard_map/ppermute | solution.py:75
  235.1 17.3 %collective-permute-start.5 = (f32[12,8,512]{2,1,0:T(8,128)S(1)}, f32[12,8,512]{2,1,0:T(8,128)S(1)}, u32[]{:S(2)}, u32[]{:S(2)}) collective-permute-start(f32[12,8,512]{2,1,0:T(8,128)S(1)} %bitcast.88), channel_id=1, source_target_pairs={{0,6},{1,7},{2,4},{3,5},{4,2},{5,3},{6,0},{7,1},{8,14},{9,15},{10,... | collective-permute-start | bytes 589832 | tf_op jit(solution)/shard_map/ppermute | solution.py:75
  238.7 17.1 %collective-permute-start.6 = (f32[12,8,512]{2,1,0:T(8,128)S(1)}, f32[12,8,512]{2,1,0:T(8,128)S(1)}, u32[]{:S(2)}, u32[]{:S(2)}) collective-permute-start(f32[12,8,512]{2,1,0:T(8,128)S(1)} %bitcast.87), channel_id=1, source_target_pairs={{0,7},{1,6},{2,5},{3,4},{4,3},{5,2},{6,1},{7,0},{8,15},{9,14},{10,... | collective-permute-start | bytes 589832 | tf_op jit(solution)/shard_map/ppermute | solution.py:75
  274.3 45.0 %reduce-scatter.5.cloned.1.call-start = ((), (), s32[]{:S(2)}) async-start(), calls=%async_computation.4 | async-start | bytes 81920 | tf_op jit(solution)/shard_map/reduce_scatter | solution.py:80
Sparse Core Ops, SparseCore 0:
  274.5 18.2 reduce-scatter.2
  295.2 24.0 reduce-scatter.4
